TPU v7x, 256 devices: a whole 4x4x8 slice. The times are simulated.
256 devices in a mesh: row: 16 (over y, x), col: 16 (over z, core).
Axes of the slice: x: 4, y: 4, z: 8, core: 2. Of those that a mesh axis runs over, the one named last changes fastest.
Arguments:
- a_vals: bfloat16 [256, 64, 256, 256], P('row', 'col'), may hold values from -0.1875 to 0.1875
- a_cols: int32 [256, 64], P('row', 'col'), may hold values from 0 to 15
- p_vals: bfloat16 [256, 256, 512], P(('row', 'col')), may hold values from -0.375 to 0.375
Outputs:
- coarse: float32 [8192, 8192], P('row', 'col')
All inputs are finite; a program needn't handle non-finite values.
Results may differ from a plain program's by a relative error of at most 0.0029.
Values may be sent and summed in bfloat16 or wider, within the bound.
A program may use at most 192 MiB of HBM per device.

v0:
```python
import jax
import jax.numpy as jnp
from jax import lax
from jax.sharding import PartitionSpec as P


def per_device(a_vals, a_cols, p_vals):
    row_count = lax.axis_size("row")
    slot_count = a_cols.shape[1]
    block_size = a_vals.shape[2]
    coarse_width = p_vals.shape[2]
    own_count = p_vals.shape[0]
    column_count = row_count * own_count
    zero_left = jnp.zeros((column_count, coarse_width, block_size), jnp.float32)
    pieces = lax.all_gather(p_vals, "col", axis=0, tiled=True)
    piece_rows = pieces.shape[0]
    products = jnp.einsum("nda,nsdb->nsab", pieces, a_vals, preferred_element_type=jnp.float32)
    products = products.reshape(piece_rows * slot_count, coarse_width, block_size)
    left_terms = (
        zero_left.at[a_cols.reshape(piece_rows * slot_count)].add(products).astype(jnp.bfloat16)
    )
    products = jnp.einsum(
        "lad,ldc->alc",
        left_terms,
        lax.all_gather(p_vals, "row", axis=0, tiled=True),
        preferred_element_type=jnp.float32,
    )
    summed = products.reshape(coarse_width, row_count, own_count, coarse_width).sum(axis=2)
    summed = summed.reshape(coarse_width, row_count * coarse_width)
    return lax.psum_scatter(summed, "col", scatter_dimension=1, tiled=True)


def solution(mesh):
    return jax.shard_map(
        per_device,
        mesh=mesh,
        in_specs=(P("row", "col", None, None), P("row", "col"), P(("row", "col"), None, None)),
        out_specs=P("row", "col"),
        check_vma=False,
    )
```

profile of v0, /device:TPU:1, one launch (start us, length us, event | category | flops | bytes accessed | tf_op | source)
XLA Modules:
  0.0 314.9 jit_solution(15966742123707560703)
XLA Ops:
  6.5 0.0 all-gather.3.cloned.1.call-start
  6.5 0.7 all-gather.3.cloned.1.call-update
  7.3 0.0 all-gather.5.cloned.1.call-start
  7.3 0.7 all-gather.5.cloned.1.call-update
  8.0 0.0 reduce-scatter.2.cloned.1.call-start
  8.1 0.8 copy.14
  8.8 0.1 reshape.41
  8.9 46.6 %all-gather.3.cloned.1.call-done = bf16[16,256,512]{2,1,0:T(8,128)(2,1)} async-done(((bf16[1,256,512]{2,1,0:T(8,128)(2,1)}), bf16[16,256,512]{2,1,0:T(8,128)(2,1)}) %all-gather.3.cloned.1.call-update) | async-done | bytes 4194320 | tf_op jit(solution)/shard_map/all_gather | solution.py:15
  55.5 16.8 %fusion = f32[16,4,256,512]{3,2,1,0:T(8,128)} fusion(bf16[16,4,256,256]{3,2,1,0:T(8,128)(2,1)} %param.3, bf16[16,256,512]{2,1,0:T(8,128)(2,1)} %all-gather.3.cloned.1.call-done), kind=kOutput, calls=%fused_computation.1 | convolution fusion | flops 4294967296 | bytes 46137344 | tf_op jit(solution)/shard_map/nda,nsdb->nsab/dot_general | solution.py:17
  72.4 33.5 %copy.16 = f32[64,512,256]{2,1,0:T(8,128)} copy(f32[64,512,256]{1,2,0:T(8,128)} %bitcast.15) | data formatting | bytes 67108864 | tf_op jit(solution)/shard_map/reshape | solution.py:18
  105.9 4.1 %broadcast_in_dim.4 = f32[16,512,256]{2,1,0:T(8,128)} broadcast(f32[]{:T(128)} %constant.3.clone.1), dimensions={} | broadcast | bytes 8388612 | tf_op jit(solution)/shard_map/broadcast_in_dim | solution.py:14
  110.0 69.8 %scatter_fusion = f32[16,512,256]{2,1,0:T(8,128)} fusion(f32[16,512,256]{2,1,0:T(8,128)} %broadcast_in_dim.4, s32[64]{0:T(128)S(1)} %fusion.4, f32[64,512,256]{2,1,0:T(8,128)} %copy.16), kind=kCustom, calls=%fused_computation | custom fusion | flops 8388608 | bytes 100663552 | tf_op jit(solution)/shard_map/scatter-add | solution.py:20
  179.8 0.0 all-gather.5.cloned.1.call-done
  179.8 12.7 %fusion.2 = f32[16,512,512]{1,2,0:T(8,128)} fusion(bf16[16,256,512]{2,1,0:T(8,128)(2,1)} %all-gather.5.cloned.1.call-done, f32[16,512,256]{2,1,0:T(8,128)} %scatter_fusion), kind=kOutput, calls=%fused_computation.3 | convolution fusion | flops 2149580800 | bytes 29360128 | tf_op jit(solution)/shard_map/lad,ldc->alc/dot_general | solution.py:22
  192.5 17.4 %copy.18 = f32[512,8192]{1,0:T(8,128)} copy(f32[512,8192]{0,1:T(8,128)} %bitcast.16) | data formatting | bytes 33554432 | tf_op jit(solution)/shard_map/reshape | solution.py:29
  210.0 0.0 reduce-scatter.2.cloned.1.call-update
  210.0 98.4 %reduce-scatter.2.cloned.1.call-done = f32[512,512]{1,0:T(8,128)} async-done(((f32[512,8192]{1,0:T(8,128)}), f32[512,512]{1,0:T(8,128)}) %reduce-scatter.2.cloned.1.call-update) | async-done | bytes 1048592 | tf_op jit(solution)/shard_map/reduce_scatter | solution.py:30
  (1 shorter events, 0.0 us)
Async XLA Ops:
  6.5 49.0 %all-gather.3.cloned.1.call-start = ((), (), s32[]{:S(2)}) async-start(), calls=%async_computation.1 | async-start | bytes 4456448 | tf_op jit(solution)/shard_map/all_gather | solution.py:15
  7.3 172.6 %all-gather.5.cloned.1.call-start = ((), (), s32[]{:S(2)}) async-start(), calls=%async_computation.2 | async-start | bytes 4456448 | tf_op jit(solution)/shard_map/all_gather | solution.py:25
  8.0 300.4 %reduce-scatter.2.cloned.1.call-start = ((), (), s32[]{:S(2)}) async-start(), calls=%async_computation.3 | async-start | bytes 17825792 | tf_op jit(solution)/shard_map/reduce_scatter | solution.py:30
Sparse Core Ops, SparseCore 0:
  9.2 46.3 all-gather.2
  58.0 54.6 all-gather.4
  210.1 98.2 reduce-scatter.1
where the time goes:
time: 316 us; the launch traced here: 315 us
  waiting for transfers between devices  146 us (46%)
  other arithmetic  69.8 us (22%)
  local copies, waits for them, and re-layouts  55.9 us (18%)
  matrix products  29.5 us (9%)
  between operations  13.1 us (4%)
    reduce_scatter x1, waiting for transfers between devices, per_device(): return lax.psum_scatter(summed, 'col', scatter_dimension=1, tiled=True)  98.4 us
    scatter-add x1, other arithmetic, per_device(): zero_left.at[a_cols.reshape(piece_rows * slot_count)].add(products)  69.8 us
    all_gather x1, waiting for transfers between devices, per_device(): pieces = lax.all_gather(p_vals, 'col', axis=0, tiled=True)  46.6 us
    reshape x1, local copies, waits for them, and re-layouts, per_device(): products.reshape(piece_rows * slot_count, coarse_width, block_size)  33.5 us
    reshape x1, local copies, waits for them, and re-layouts, per_device(): summed = summed.reshape(coarse_width, row_count * coarse_width)  17.4 us
    dot_general x1, matrix products, per_device(): jnp.einsum('nda,nsdb->nsab', pieces, a_vals, preferred_element_type=jnp.f...  16.8 us
    dot_general x1, matrix products, per_device(): jnp.einsum('lad,ldc->alc', left_terms, lax.all_gather(p_vals, 'row', axis...  12.7 us
  transfers between devices with their start and end apart: 3, of which 2 were waited for; matrix products, arithmetic and copies ran while one was open for 40% of the time, Pallas kernels for 0%

commit v1 on v0

v1 whole, which is shorter than its diff:
```python
import functools

import jax
import jax.numpy as jnp
from jax import lax
from jax.experimental import pallas as pl
from jax.experimental.pallas import tpu as pltpu
from jax.sharding import PartitionSpec as P

MESH = pl.DeviceIdType.MESH
NX, NY, NZ = 4, 4, 8
T = 256
SLOTS = 4
ROWS = 16
NSLOT = ROWS * SLOTS
F32 = jnp.float32
BF16 = jnp.bfloat16


def place():
    row, col = lax.axis_index("row"), lax.axis_index("col")
    return row // NX, row % NX, col // 2, col % 2


def chain(a_cols):
    _, _, z, core = place()
    slot = lax.broadcasted_iota(jnp.int32, (1, NSLOT), 1)
    owner = slot // SLOTS
    dist = (owner // 2 - z + NZ) % NZ
    back = jnp.where(dist > NZ // 2, 1, 0)
    near = jnp.minimum(dist, NZ - dist)
    order = ((near * 2 + back) * 2 + (owner + core) % 2) * SLOTS + slot % SLOTS
    cols = a_cols.reshape(1, NSLOT)
    asked = jnp.concatenate([cols.reshape(NSLOT, 1), jnp.arange(16, dtype=jnp.int32).reshape(16, 1)], 0)
    before = jnp.concatenate([order.reshape(NSLOT, 1), jnp.full((16, 1), 1024, jnp.int32)], 0)
    hit = (cols == asked) & (order < before)
    best = jnp.max(jnp.where(hit, order * NSLOT + slot, -1), axis=1)
    return jnp.where(best < 0, NSLOT, best % NSLOT)


def kernel(link_ref, a_hbm, p_hbm, out_ref, run, a, pt, pc, xr, rcv, acc,
           load_sem, zs, zr, hs, hr, ws, wr, xs_sem, xr_sem, ss, sr):
    y, x, z, core = place()
    row, col = y * NX + x, z * 2 + core

    def zdev(step):
        return (row, ((z + step + NZ) % NZ) * 2 + core)

    def sibling():
        return (row, z * 2 + (1 - core))

    def xdev(step):
        return (y * NX + (x + step + NX) % NX, col)

    def ydev(step):
        return (((y + step + NY) % NY) * NX + x, col)

    load_p = [
        pltpu.make_async_copy(p_hbm.at[0, :, pl.ds(n * T, T)], pc.at[row, n], load_sem.at[n]) for n in range(2)
    ]
    for c in load_p:
        c.start()
    load_a = pltpu.make_async_copy(a_hbm, a, load_sem.at[2])
    load_a.start()

    barrier = pltpu.get_barrier_semaphore()
    partners = [zdev(1), zdev(-1), sibling(), xdev(1), xdev(-1), ydev(1), ydev(-1)]
    for dev in partners:
        pl.semaphore_signal(barrier, inc=1, device_id=dev, device_id_type=MESH)
    run[NSLOT] = jnp.zeros((2, T, T), F32)
    for n in range(2):
        load_p[n].wait()
        pt[col, n] = pc[row, n].T
    pl.semaphore_wait(barrier, len(partners))

    sends = []

    def copy(ref, send_sem, recv_sem, dev, dst=None):
        return pltpu.make_async_remote_copy(
            src_ref=ref, dst_ref=ref if dst is None else dst, send_sem=send_sem, recv_sem=recv_sem,
            device_id=dev, device_id_type=MESH,
        )

    def send(*args, **kw):
        c = copy(*args, **kw)
        c.start()
        sends.append(c)

    def zmsg(e, d, hop, recv):
        sign = 1 - 2 * d
        back = hop + 1 if recv else hop
        tile = ((z - sign * back + 2 * NZ) % NZ) * 2 + core
        ref = pt.at[tile, e] if hop < 3 else pt.at[tile, e, pl.ds(d * (T // 2), T // 2)]
        i = (e * 2 + d) * 4 + hop
        return ref, zs.at[i], zr.at[i], zdev(sign)

    def zsend(e, d, hop):
        send(*zmsg(e, d, hop, False))

    def zwait(e, d, hop):
        copy(*zmsg(e, d, hop, True)).wait_recv()

    def hmsg(e, shift, recv):
        tile = ((z + shift + NZ) % NZ) * 2 + ((1 - core) if recv else core)
        i = e * 8 + (shift + NZ) % NZ
        return pt.at[tile, e], hs.at[i], hr.at[i], sibling()

    def hsend(e, shift):
        send(*hmsg(e, shift, False))

    def hwait(e, shift):
        copy(*hmsg(e, shift, True)).wait_recv()

    names = {}

    def wid(name):
        return names.setdefault(name, len(names))

    def wmsg(name, dy, dx, part, dev):
        tile = ((y + dy + 2 * NY) % NY) * NX + (x + dx + 2 * NX) % NX
        ref = pc.at[tile]
        if part is not None:
            n, q = part
            ref = ref.at[n] if q is None else ref.at[n, pl.ds(q * (T // 2), T // 2)]
        i = wid(name)
        return ref, ws.at[i], wr.at[i], dev

    def step_of(axis, amount):
        return (0, amount) if axis == 0 else (amount, 0)

    def wdev(axis, d):
        return xdev(1 - 2 * d) if axis == 0 else ydev(1 - 2 * d)

    def wgo(name, axis, d, offset, part, recv):
        dy, dx = offset
        if recv:
            sy, sx = step_of(axis, -(1 - 2 * d))
            dy, dx = dy + sy, dx + sx
        m = wmsg(name, dy, dx, part, wdev(axis, d))
        if recv:
            copy(*m).wait_recv()
        else:
            send(*m)

    def w_own(axis, d, recv):
        wgo(("own", axis, d), axis, d, (0, 0), None, recv)

    def w_line2(axis, d, n, recv):
        wgo(("line2", axis, d, n), axis, d, step_of(axis, -(1 - 2 * d)), (n, d), recv)

    def w_diag(axis, d, o, recv):
        wgo(("diag", axis, d, o), axis, d, step_of(1 - axis, o), (1 - axis, None), recv)

    def w_diag2(axis, d, o, recv):
        ay, ax = step_of(axis, -(1 - 2 * d))
        by, bx = step_of(1 - axis, o)
        wgo(("diag2", axis, d, o), axis, d, (ay + by, ax + bx), (1 - axis, d), recv)

    both = [(axis, d) for axis in range(2) for d in range(2)]

    def left(dist, tiles):
        @pl.loop(0, tiles * SLOTS)
        def _(q):
            m = q // SLOTS
            tile = ((z + dist * (1 - 2 * (m // 2)) + NZ) % NZ) * 2 + (core + m) % 2
            s = tile * SLOTS + q % SLOTS
            prev = link_ref[s]
            for e in range(2):
                run[s, e] = run[prev, e] + jnp.dot(pt[tile, e], a[s], preferred_element_type=F32)

    for e in range(2):
        for d in range(2):
            zsend(e, d, 0)
        hsend(e, 0)
    for axis, d in both:
        w_own(axis, d, False)
    for e in range(2):
        for d in range(2):
            zwait(e, d, 0)
            zsend(e, d, 1)
        for d in range(2):
            hsend(e, -(1 - 2 * d))
    load_a.wait()
    for axis, d in both:
        w_own(axis, d, True)
    for axis, d in both:
        for n in range(2):
            w_line2(axis, d, n, False)
    for o in (-1, 1):
        for axis, d in both:
            w_diag(axis, d, o, False)
    for e in range(2):
        hwait(e, 0)
    left(0, 2)
    for e in range(2):
        for d in range(2):
            zwait(e, d, 1)
            zsend(e, d, 2)
        for d in range(2):
            hsend(e, -2 * (1 - 2 * d))
    for e in range(2):
        for d in range(2):
            hwait(e, 1 - 2 * d)
    left(1, 4)
    for axis, d in both:
        for n in range(2):
            w_line2(axis, d, n, True)
    for axis, d in both:
        w_diag(axis, d, 2, False)
    for e in range(2):
        for d in range(2):
            zwait(e, d, 2)
            zsend(e, d, 3)
        for d in range(2):
            hsend(e, -3 * (1 - 2 * d))
    for o in (-1, 1):
        for axis, d in both:
            w_diag(axis, d, o, True)
            w_diag2(axis, d, o, False)
    for e in range(2):
        for d in range(2):
            hwait(e, 2 * (1 - 2 * d))
    left(2, 4)
    for axis, d in both:
        w_diag(axis, d, 2, True)
        w_diag2(axis, d, 2, False)
    for e in range(2):
        for d in range(2):
            hwait(e, 3 * (1 - 2 * d))
    left(3, 4)
    for e in range(2):
        for d in range(2):
            zwait(e, d, 3)
        hsend(e, 4)
    for o in (-1, 1, 2):
        for axis, d in both:
            w_diag2(axis, d, o, True)
    for e in range(2):
        hwait(e, 4)
    left(4, 2)

    def product(block, q):
        last = link_ref[NSLOT + block]
        lhs = run[last, q % 2].astype(BF16)
        return jnp.dot(lhs, pc[block, q // 2], preferred_element_type=F32)

    def block_of(shift, k):
        return ((z + shift + NZ) % NZ) * 2 + k

    def exchange(shift):
        block = block_of(shift, 1 - core)
        m = (shift + NZ) % NZ
        base = m * 4

        @pl.loop(0, 4)
        def _(q):
            a[base + q] = product(block, q).astype(BF16)

        send(a.at[pl.ds(base, 4)], xs_sem.at[m], xr_sem.at[m], sibling(), dst=xr.at[pl.ds(base, 4)])

    def exchange_wait(shift):
        m = (shift + NZ) % NZ
        ref = xr.at[pl.ds(m * 4, 4)]
        copy(ref, xs_sem.at[m], xr_sem.at[m], sibling()).wait_recv()

    def own(shift, d):
        block = block_of(shift, core)
        m = (shift + NZ) % NZ
        exchange_wait(shift)

        @pl.loop(0, 4)
        def _(q):
            acc[d * 4 + q] = product(block, q) + xr[m * 4 + q].astype(F32)

    def rsend(d, hop, q):
        i = (d * 4 + hop) * 4 + q
        send(a.at[32 + i], ss.at[i], sr.at[i], zdev(1 - 2 * d), dst=rcv.at[i])

    def rwait(d, hop, q):
        i = (d * 4 + hop) * 4 + q
        copy(rcv.at[i], ss.at[i], sr.at[i], zdev(1 - 2 * d)).wait_recv()
        return rcv[i].astype(F32)

    exchange(4)
    exchange(3)
    exchange(-3)
    own(4, 0)
    for q in range(2):
        for d in range(2):
            t = 2 * d + q
            a[32 + d * 16 + t] = acc[t].astype(BF16)
            rsend(d, 0, t)
    for shift in (2, -2, 1, -1, 0):
        exchange(shift)
    for hop in range(1, 4):
        for d in range(2):
            own((4 - hop) * (1 - 2 * d), d)
        for step in range(4):
            for d in range(2):
                q = (2 + step) % 4 if d == 0 else step
                total = acc[d * 4 + q]
                if hop > 1 or step >= 2:
                    total = total + rwait(d, hop - 1, q)
                a[32 + (d * 4 + hop) * 4 + q] = total.astype(BF16)
                rsend(d, hop, q)
    own(0, 0)
    for step in range(4):
        for d in range(2):
            q = (2 + step) % 4 if d == 0 else step
            acc[q] = acc[q] + rwait(d, 3, q)
    for q in range(4):
        out_ref[pl.ds((q % 2) * T, T), pl.ds((q // 2) * T, T)] = acc[q]
    for c in sends:
        c.wait_send()


def per_device(a_vals, a_cols, p_vals):
    links = chain(a_cols)
    dma = pltpu.SemaphoreType.DMA
    return pl.pallas_call(
        kernel,
        out_shape=jax.ShapeDtypeStruct((2 * T, 2 * T), F32),
        in_specs=[
            pl.BlockSpec(memory_space=pltpu.SMEM),
            pl.BlockSpec(memory_space=pl.ANY),
            pl.BlockSpec(memory_space=pl.ANY),
        ],
        out_specs=pl.BlockSpec(memory_space=pltpu.VMEM),
        scratch_shapes=[
            pltpu.VMEM((NSLOT + 1, 2, T, T), F32),
            pltpu.VMEM((NSLOT, T, T), BF16),
            pltpu.VMEM((ROWS, 2, T, T), BF16),
            pltpu.VMEM((ROWS, 2, T, T), BF16),
            pltpu.VMEM((32, T, T), BF16),
            pltpu.VMEM((32, T, T), BF16),
            pltpu.VMEM((8, T, T), F32),
            dma((3,)),
            dma((16,)), dma((16,)),
            dma((16,)), dma((16,)),
            dma((36,)), dma((36,)),
            dma((8,)), dma((8,)),
            dma((32,)), dma((32,)),
        ],
        compiler_params=pltpu.CompilerParams(
            collective_id=0, has_side_effects=True, vmem_limit_bytes=62 * 1024 * 1024
        ),
        cost_estimate=pl.CostEstimate(flops=6_442_450_944, bytes_accessed=10_000_000, transcendentals=0),
    )(links, a_vals.reshape(NSLOT, T, T), p_vals)


def solution(mesh):
    return jax.shard_map(
        per_device,
        mesh=mesh,
        in_specs=(P("row", "col", None, None), P("row", "col"), P(("row", "col"), None, None)),
        out_specs=P("row", "col"),
        check_vma=False,
    )
```

time: 316 us -> 94.4 us (0.30)
  waiting for transfers between devices: 146 us -> 0 us
  Pallas kernels: 0 us -> 90.3 us
  other arithmetic: 69.8 us -> 0.77 us
  local copies, waits for them, and re-layouts: 55.9 us -> 3.2 us
  matrix products: 29.5 us -> 0 us
  between operations: 13.1 us -> 0.02 us
    reduce_scatter x1 -> x0, waiting for transfers between devices: 98.4 us -> none  [per_device(): return lax.psum_scatter(summed, 'col', scatter_dimension=1, tiled=True)]
    pallas_call x0 -> x1, Pallas kernels: none -> 90.3 us  [per_device(): pl.pallas_call(kernel, out_shape=jax.ShapeDtypeStruct((2 * T, 2 * T), F32...]
    scatter-add x1 -> x0, other arithmetic: 69.8 us -> none  [per_device(): zero_left.at[a_cols.reshape(piece_rows * slot_count)].add(products)]
    reshape x3 -> x0, local copies, waits for them, and re-layouts: 51.1 us -> none  [the longest x1 33.5 us: per_device(): products.reshape(piece_rows * slot_count, coarse_width, block_size)]
    all_gather x2 -> x0, waiting for transfers between devices: 46.6 us -> none  [the longest x1 46.6 us: per_device(): pieces = lax.all_gather(p_vals, 'col', axis=0, tiled=True)]
    dot_general x2 -> x0, matrix products: 29.5 us -> none  [the longest x1 16.8 us: per_device(): jnp.einsum('nda,nsdb->nsab', pieces, a_vals, preferred_element_type=jnp.f...]
    broadcast_in_dim x1 -> x0, local copies, waits for them, and re-layouts: 4.09 us -> none  [per_device(): zero_left = jnp.zeros((column_count, coarse_width, block_size), jnp.float32)]
  transfers between devices with their start and end apart: 3 -> 0, of which waited for: 2 -> 0; matrix products, arithmetic and copies ran while one was open for 40% -> 0% of each run, Pallas kernels for 0% -> 0%
where the time goes in v1:
time: 94.4 us; the launch traced here: 94.2 us
  Pallas kernels  90.3 us (96%)
  local copies, waits for them, and re-layouts  3.2 us (3%)
    pallas_call x1, Pallas kernels, per_device(): pl.pallas_call(kernel, out_shape=jax.ShapeDtypeStruct((2 * T, 2 * T), F32...  90.3 us
    unnamed x2, local copies, waits for them, and re-layouts  3.02 us

profile of v1, /device:TPU:1, one launch (start us, length us, event | category | flops | bytes accessed | tf_op | source)
XLA Modules:
  0.0 94.2 jit_solution(11331038117903109779)
XLA Ops:
  0.1 0.8 copy.8
  0.8 0.1 reshape_reshape.3
  0.9 0.1 eq.25
  1.0 0.1 add_bitcast_fusion
  1.1 0.1 select_reduce_fusion
  1.2 0.5 compare_select_fusion.10.link_ref
  1.7 90.3 %shard_map.37 = f32[512,512]{1,0:T(8,128)} custom-call(s32[80]{0:T(128)} %compare_select_fusion.10.link_ref, bf16[64,256,256]{2,1,0:T(8,128)(2,1)} %bitcast.5, bf16[1,256,512]{2,1,0:T(8,128)(2,1)} %p_hbm.1), custom_call_target="tpu_custom_call" | custom-call | flops 6442450944 | bytes 10000000 | tf_op jit(solution)/shard_map/pallas_call | solution.py:320
  92.0 2.3 %copy.11 = f32[512,512]{1,0:T(8,128)} copy(f32[512,512]{1,0:T(8,128)} %shard_map.37) | data formatting | bytes 2097152
  (3 shorter events, 0.1 us)

commit v2 on v0

v2 whole, which is shorter than its diff:
```python
import functools

import jax
import jax.numpy as jnp
from jax import lax
from jax.experimental import pallas as pl
from jax.experimental.pallas import tpu as pltpu
from jax.sharding import PartitionSpec as P

MESH = pl.DeviceIdType.MESH
NX, NY, NZ = 4, 4, 8
T = 256
SLOTS = 4
ROWS = 16
NSLOT = ROWS * SLOTS
HALF, QUART = T // 2, T // 4
UNITS = ((0, 0), (1, 0), (0, 1), (1, 1))
F32 = jnp.float32
BF16 = jnp.bfloat16


def place():
    row, col = lax.axis_index("row"), lax.axis_index("col")
    return row // NX, row % NX, col // 2, col % 2


def chain(cols_ref, links_ref, z, core):
    def order_of(owner, k):
        dist = (owner // 2 - z + NZ) % NZ
        back = jnp.where(dist > NZ // 2, 1, 0)
        near = jnp.minimum(dist, NZ - dist)
        return ((near * 2 + back) * 2 + (owner + core) % 2) * SLOTS + k

    shape = (ROWS, ROWS)
    down = lax.broadcasted_iota(jnp.int32, shape, 0)
    across = lax.broadcasted_iota(jnp.int32, shape, 1)
    turned = [jnp.broadcast_to(cols_ref[k:k + 1, :], shape) for k in range(SLOTS)]
    cols = [jnp.broadcast_to(jnp.sum(jnp.where(down == across, c, 0), axis=1, keepdims=True), shape) for c in turned]
    for k in range(SLOTS + 1):
        asked = cols[k] if k < SLOTS else down
        before = order_of(down, k) if k < SLOTS else jnp.full(shape, 1024, jnp.int32)
        best = jnp.full(shape, -1, jnp.int32)
        for j in range(SLOTS):
            order = order_of(across, j)
            hit = (turned[j] == asked) & (order < before)
            best = jnp.maximum(best, jnp.where(hit, order * NSLOT + across * SLOTS + j, -1))
        best = jnp.max(best, axis=1, keepdims=True)
        links_ref[:, k:k + 1] = jnp.where(best < 0, NSLOT, best % NSLOT)


def kernel(cols_hbm, a_hbm, p_hbm, out_hbm, out_ref, run, a, pt, pc, xr, rcv, first, acc, cols, links, link_ref,
           load_sem, out_sem, zs, zr, hs, hr, ws, wr, xs_sem, xr_sem, ss, sr):
    y, x, z, core = place()
    row, col = y * NX + x, z * 2 + core

    def zdev(step):
        return (row, ((z + step + NZ) % NZ) * 2 + core)

    def sibling():
        return (row, z * 2 + (1 - core))

    def xdev(step):
        return (y * NX + (x + step + NX) % NX, col)

    def ydev(step):
        return (((y + step + NY) % NY) * NX + x, col)

    load_p = [
        pltpu.make_async_copy(p_hbm.at[0, :, pl.ds(n * T, T)], pc.at[n, row], load_sem.at[n]) for n in range(2)
    ]
    for c in load_p:
        c.start()
    load_cols = pltpu.make_async_copy(cols_hbm, cols, load_sem.at[3])
    load_cols.start()
    load_a = pltpu.make_async_copy(a_hbm, a, load_sem.at[2])
    load_a.start()

    barrier = pltpu.get_barrier_semaphore()
    partners = [zdev(1), zdev(-1), sibling(), xdev(1), xdev(-1), ydev(1), ydev(-1)]
    for dev in partners:
        pl.semaphore_signal(barrier, inc=1, device_id=dev, device_id_type=MESH)
    for e in range(2):
        run[e, NSLOT] = jnp.zeros((T, T), F32)
        load_p[e].wait()
        pt[e, col] = pc[e, row].T
    pl.semaphore_wait(barrier, len(partners))

    result = []
    late = []
    held = ([], [])

    def copy(ref, send_sem, recv_sem, dev, dst=None):
        return pltpu.make_async_remote_copy(
            src_ref=ref, dst_ref=ref if dst is None else dst, send_sem=send_sem, recv_sem=recv_sem,
            device_id=dev, device_id_type=MESH,
        )

    def send(into, *args, **kw):
        c = copy(*args, **kw)
        c.start()
        into.append(c)

    def zmsg(e, d, hop, q, recv):
        sign = 1 - 2 * d
        back = hop + 1 if recv else hop
        tile = ((z - sign * back + 2 * NZ) % NZ) * 2 + core
        i = ((e * 2 + d) * 4 + hop) * 2 + q
        return pt.at[e, tile, pl.ds(q * HALF, HALF)], zs.at[i], zr.at[i], zdev(sign)

    def zsend(e, hop, k):
        for d in range(2):
            send(held[e], *zmsg(e, d, hop, (d + k) % 2, False))

    def zwait(e, hop, k):
        for d in range(2):
            copy(*zmsg(e, d, hop, (d + k) % 2, True)).wait_recv()

    def hmsg(e, shift, recv):
        tile = ((z + shift + NZ) % NZ) * 2 + ((1 - core) if recv else core)
        i = e * 8 + (shift + NZ) % NZ
        return pt.at[e, tile], hs.at[i], hr.at[i], sibling()

    def hsend(e, *shifts):
        for shift in shifts:
            send(held[e], *hmsg(e, shift, False))

    def hwait(e, *shifts):
        for shift in shifts:
            copy(*hmsg(e, shift, True)).wait_recv()

    names = {}

    def step_of(axis, amount):
        return (0, amount) if axis == 0 else (amount, 0)

    def wgo(name, axis, d, offset, rows, recv):
        sign = 1 - 2 * d
        dy, dx = offset
        if recv:
            sy, sx = step_of(axis, -sign)
            dy, dx = dy + sy, dx + sx
        tile = ((y + dy + 2 * NY) % NY) * NX + (x + dx + 2 * NX) % NX
        ref = pc.at[name[0], tile]
        if rows is not None:
            ref = ref.at[pl.ds(*rows)]
        i = names.setdefault((axis, d) + name, len(names))
        m = (ref, ws.at[i], wr.at[i], xdev(sign) if axis == 0 else ydev(sign))
        if recv:
            copy(*m).wait_recv()
        else:
            send(late, *m)

    both = [(axis, d) for axis in range(2) for d in range(2)]

    def w_own(n, recv):
        for axis, d in both:
            wgo((n, "own"), axis, d, (0, 0), None, recv)

    def w_line2(n, recv):
        for axis, d in both:
            for f in range(2):
                wgo((n, "line2", f), axis, d, step_of(axis, 2 * d - 1), (f * HALF + d * QUART, QUART), recv)

    def w_diag(n, o, recv):
        for axis, d in both:
            wgo((n, "diag", o), axis, d, step_of(1 - axis, o), ((1 - axis) * HALF, HALF), recv)

    def w_diag2(n, o, recv):
        for axis, d in both:
            ay, ax = step_of(axis, 2 * d - 1)
            by, bx = step_of(1 - axis, o)
            wgo((n, "diag2", o), axis, d, (ay + by, ax + bx), ((1 - axis) * HALF + d * QUART, QUART), recv)

    def left(e, dist, lo, hi):
        @pl.loop(lo, hi)
        def _(m):
            tile = ((z + dist * (1 - 2 * (m // 2)) + NZ) % NZ) * 2 + (core + m) % 2
            for k in range(SLOTS):
                s = tile * SLOTS + k
                prev = link_ref[tile, k]
                run[e, s] = run[e, prev] + jnp.dot(pt[e, tile], a[s], preferred_element_type=F32)

    def product(e, n, block):
        last = link_ref[block, SLOTS]
        return jnp.dot(run[e, last].astype(BF16), pc[n, block], preferred_element_type=F32)

    def block_of(shift, k):
        return ((z + shift + NZ) % NZ) * 2 + k

    def xmsg(u, shift):
        m = (shift + NZ) % NZ
        e, n = UNITS[u]
        i = u * 8 + m
        return pt.at[e, n * 8 + m], xs_sem.at[i], xr_sem.at[i], sibling(), xr.at[i]

    def exchange(u, *shifts):
        e, n = UNITS[u]
        for shift in shifts:
            pt[e, n * 8 + (shift + NZ) % NZ] = product(e, n, block_of(shift, 1 - core)).astype(BF16)
            send(late, *xmsg(u, shift))

    def own(u, shift):
        e, n = UNITS[u]
        value = product(e, n, block_of(shift, core))
        copy(*xmsg(u, shift)).wait_recv()
        return value + xr[u * 8 + (shift + NZ) % NZ].astype(F32)

    def rmsg(u, d, hop, r):
        i = (u * 2 + d) * 4 + hop
        buf = first.at[i] if u == 0 else a.at[i - 8]
        rows = pl.ds(r * HALF, HALF)
        return buf.at[rows], ss.at[i * 2 + r], sr.at[i * 2 + r], zdev(1 - 2 * d), rcv.at[i, rows]

    def pass_on(u, d, hop, r, value):
        m = rmsg(u, d, hop, r)
        m[0][...] = value.astype(BF16)
        send(late, *m)

    def arrived(u, d, hop, r):
        copy(*rmsg(u, d, hop, r)).wait_recv()
        return rcv[(u * 2 + d) * 4 + hop, pl.ds(r * HALF, HALF)].astype(F32)

    def ring(u, step):
        e, n = UNITS[u]
        slot = u * 2
        hop = (step + 1) // 2
        if step == 0:
            total = own(u, 4)
            for d in range(2):
                pass_on(u, d, 0, d, total[d * HALF:(d + 1) * HALF])
            return
        if step == 7:
            out_ref[pl.ds(e * T, T), pl.ds(n * T, T)] = own(u, 0)
        elif step % 2 == 1:
            for d in range(2):
                acc[slot + d] = own(u, (4 - hop) * (1 - 2 * d))
        for d in range(2):
            r = 1 - d if step % 2 == 1 else d
            if step >= 7:
                rows = pl.ds(e * T + r * HALF, HALF), pl.ds(n * T, T)
                out_ref[rows] = out_ref[rows] + arrived(u, d, 3, r)
                continue
            total = acc[slot + d, pl.ds(r * HALF, HALF)]
            if step > 1:
                total = total + arrived(u, d, hop - 1, r)
            pass_on(u, d, hop, r, total)
        if step == 8:
            tile = pl.ds(e * T, T), pl.ds(n * T, T)
            result.append(pltpu.make_async_copy(out_ref.at[tile], out_hbm.at[tile], out_sem.at[u]))
            result[-1].start()

    zsend(0, 0, 0)
    zsend(0, 0, 1)
    hsend(0, 0)
    w_own(0, False)
    zsend(1, 0, 0)
    zsend(1, 0, 1)
    hsend(1, 0)
    load_cols.wait()
    chain(cols, links, z, core)
    to_scalars = pltpu.make_async_copy(links, link_ref, load_sem.at[4])
    to_scalars.start()
    load_a.wait()
    to_scalars.wait()
    zwait(0, 0, 0)
    zsend(0, 1, 0)
    zwait(0, 0, 1)
    zsend(0, 1, 1)
    hsend(0, 1, -1)
    w_own(0, True)
    w_line2(0, False)
    w_diag(0, -1, False)
    w_diag(0, 1, False)
    zwait(1, 0, 0)
    zsend(1, 1, 0)
    zwait(1, 0, 1)
    zsend(1, 1, 1)
    hsend(1, 1, -1)
    hwait(0, 0)
    left(0, 0, 0, 2)
    hwait(1, 0)
    left(1, 0, 0, 2)
    zwait(0, 1, 0)
    zsend(0, 2, 0)
    zwait(0, 1, 1)
    zsend(0, 2, 1)
    hsend(0, 2, -2)
    w_line2(0, True)
    w_diag(0, 2, False)
    w_own(1, False)
    hwait(0, 1, -1)
    left(0, 1, 0, 4)
    zwait(1, 1, 0)
    zsend(1, 2, 0)
    zwait(1, 1, 1)
    zsend(1, 2, 1)
    hsend(1, 2, -2)
    w_diag(0, -1, True)
    w_diag(0, 1, True)
    w_diag2(0, -1, False)
    w_diag2(0, 1, False)
    hwait(1, 1, -1)
    left(1, 1, 0, 4)
    zwait(0, 2, 0)
    zsend(0, 3, 0)
    w_diag(0, 2, True)
    w_diag2(0, 2, False)
    zwait(0, 2, 1)
    hsend(0, 3, -3)
    hwait(0, 2, -2)
    left(0, 2, 0, 4)
    zwait(1, 2, 0)
    zsend(1, 3, 0)
    zwait(1, 2, 1)
    hsend(1, 3, -3)
    hwait(0, 3, -3)
    left(0, 3, 0, 4)
    zwait(0, 3, 0)
    hsend(0, 4)
    left(0, 4, 0, 1)
    w_diag2(0, -1, True)
    w_diag2(0, 1, True)
    w_diag2(0, 2, True)
    hwait(0, 4)
    left(0, 4, 1, 2)
    for c in held[0]:
        c.wait_send()
    exchange(0, 4, 3, -3)
    hwait(1, 2, -2)
    left(1, 2, 0, 4)
    ring(0, 0)
    ring(0, 1)
    zwait(1, 3, 0)
    hsend(1, 4)
    hwait(1, 3, -3)
    left(1, 3, 0, 4)
    left(1, 4, 0, 1)
    hwait(1, 4)
    left(1, 4, 1, 2)
    for c in held[1]:
        c.wait_send()
    exchange(1, 4, 3, -3)
    w_own(1, True)
    w_line2(1, False)
    w_diag(1, -1, False)
    w_diag(1, 1, False)
    exchange(0, 2, -2)
    ring(1, 0)
    ring(1, 1)
    ring(0, 2)
    ring(0, 3)
    exchange(1, 2, -2)
    w_line2(1, True)
    w_diag(1, 2, False)
    exchange(0, 1, -1)
    ring(1, 2)
    ring(1, 3)
    w_diag(1, -1, True)
    w_diag(1, 1, True)
    w_diag2(1, -1, False)
    w_diag2(1, 1, False)
    ring(0, 4)
    w_diag(1, 2, True)
    w_diag2(1, 2, False)
    exchange(1, 1, -1)
    ring(0, 5)
    ring(0, 6)
    w_diag2(1, -1, True)
    w_diag2(1, 1, True)
    w_diag2(1, 2, True)

    exchange(2, 4, 3, -3)
    ring(1, 4)
    ring(2, 0)
    exchange(3, 4, 3, -3)
    ring(2, 1)
    exchange(2, 2, -2)
    ring(3, 0)
    ring(3, 1)
    exchange(3, 2, -2)
    ring(1, 5)
    exchange(0, 0)
    ring(2, 2)
    ring(3, 2)
    exchange(2, 1, -1)
    ring(1, 6)
    ring(2, 3)
    exchange(3, 1, -1)
    ring(3, 3)
    exchange(1, 0)
    ring(0, 7)
    ring(0, 8)
    exchange(2, 0)
    ring(2, 4)
    ring(3, 4)
    exchange(3, 0)
    ring(2, 5)
    ring(3, 5)
    ring(1, 7)
    ring(1, 8)
    ring(2, 6)
    ring(3, 6)
    ring(2, 7)
    ring(3, 7)
    ring(2, 8)
    ring(3, 8)
    for c in late:
        c.wait_send()
    for c in result:
        c.wait()


def per_device(a_vals, a_cols, p_vals):
    dma = pltpu.SemaphoreType.DMA
    return pl.pallas_call(
        kernel,
        out_shape=jax.ShapeDtypeStruct((2 * T, 2 * T), F32),
        in_specs=[
            pl.BlockSpec(memory_space=pl.ANY),
            pl.BlockSpec(memory_space=pl.ANY),
            pl.BlockSpec(memory_space=pl.ANY),
        ],
        out_specs=pl.BlockSpec(memory_space=pl.ANY),
        scratch_shapes=[
            pltpu.VMEM((2 * T, 2 * T), F32),
            pltpu.VMEM((2, NSLOT + 1, T, T), F32),
            pltpu.VMEM((NSLOT, T, T), BF16),
            pltpu.VMEM((2, ROWS, T, T), BF16),
            pltpu.VMEM((2, ROWS, T, T), BF16),
            pltpu.VMEM((32, T, T), BF16),
            pltpu.VMEM((32, T, T), BF16),
            pltpu.VMEM((8, T, T), BF16),
            pltpu.VMEM((8, T, T), F32),
            pltpu.VMEM((SLOTS, ROWS), jnp.int32),
            pltpu.VMEM((ROWS, 128), jnp.int32),
            pltpu.SMEM((ROWS, 128), jnp.int32),
            dma((5,)), dma((4,)),
            dma((32,)), dma((32,)),
            dma((16,)), dma((16,)),
            dma((72,)), dma((72,)),
            dma((32,)), dma((32,)),
            dma((64,)), dma((64,)),
        ],
        compiler_params=pltpu.CompilerParams(
            collective_id=0, has_side_effects=True, vmem_limit_bytes=62 * 1024 * 1024
        ),
        cost_estimate=pl.CostEstimate(flops=6_442_450_944, bytes_accessed=10_000_000, transcendentals=0),
    )(a_cols.T, a_vals.reshape(NSLOT, T, T), p_vals)


def solution(mesh):
    return jax.shard_map(
        per_device,
        mesh=mesh,
        in_specs=(P("row", "col", None, None), P("row", "col"), P(("row", "col"), None, None)),
        out_specs=P("row", "col"),
        check_vma=False,
    )
```

time: 316 us -> 84.5 us (0.27)
  waiting for transfers between devices: 146 us -> 0 us
  Pallas kernels: 0 us -> 82.1 us
  other arithmetic: 69.8 us -> 0 us
  local copies, waits for them, and re-layouts: 55.9 us -> 2.26 us
  matrix products: 29.5 us -> 0 us
  between operations: 13.1 us -> 0.01 us
    reduce_scatter x1 -> x0, waiting for transfers between devices: 98.4 us -> none  [per_device(): return lax.psum_scatter(summed, 'col', scatter_dimension=1, tiled=True)]
    pallas_call x0 -> x1, Pallas kernels: none -> 82.1 us  [per_device(): pl.pallas_call(kernel, out_shape=jax.ShapeDtypeStruct((2 * T, 2 * T), F32...]
    scatter-add x1 -> x0, other arithmetic: 69.8 us -> none  [per_device(): zero_left.at[a_cols.reshape(piece_rows * slot_count)].add(products)]
    reshape x3 -> x0, local copies, waits for them, and re-layouts: 51.1 us -> none  [the longest x1 33.5 us: per_device(): products.reshape(piece_rows * slot_count, coarse_width, block_size)]
    all_gather x2 -> x0, waiting for transfers between devices: 46.6 us -> none  [the longest x1 46.6 us: per_device(): pieces = lax.all_gather(p_vals, 'col', axis=0, tiled=True)]
    dot_general x2 -> x0, matrix products: 29.5 us -> none  [the longest x1 16.8 us: per_device(): jnp.einsum('nda,nsdb->nsab', pieces, a_vals, preferred_element_type=jnp.f...]
    broadcast_in_dim x1 -> x0, local copies, waits for them, and re-layouts: 4.09 us -> none  [per_device(): zero_left = jnp.zeros((column_count, coarse_width, block_size), jnp.float32)]
  transfers between devices with their start and end apart: 3 -> 0, of which waited for: 2 -> 0; matrix products, arithmetic and copies ran while one was open for 40% -> 0% of each run, Pallas kernels for 0% -> 0%
where the time goes in v2:
time: 84.5 us; the launch traced here: 84.3 us
  Pallas kernels  82.1 us (97%)
  local copies, waits for them, and re-layouts  2.26 us (3%)
    pallas_call x1, Pallas kernels, per_device(): pl.pallas_call(kernel, out_shape=jax.ShapeDtypeStruct((2 * T, 2 * T), F32...  82.1 us
    unnamed x1, local copies, waits for them, and re-layouts  2.26 us

profile of v2, /device:TPU:1, one launch (start us, length us, event | category | flops | bytes accessed | tf_op | source)
XLA Modules:
  0.0 84.3 jit_solution(1407366701184926200)
XLA Ops:
  0.0 82.1 %shard_map.37 = f32[512,512]{1,0:T(8,128)} custom-call(s32[4,16]{1,0:T(4,128)} %bitcast.3, bf16[64,256,256]{2,1,0:T(8,128)(2,1)} %bitcast.2, bf16[1,256,512]{2,1,0:T(8,128)(2,1)} %p_hbm.1), custom_call_target="tpu_custom_call" | custom-call | flops 6442450944 | bytes 10000000 | tf_op jit(solution)/shard_map/pallas_call | solution.py:415
  82.1 2.3 %copy.5 = f32[512,512]{1,0:T(8,128)} copy(f32[512,512]{1,0:T(8,128)} %shard_map.37) | data formatting | bytes 2097152

commit v3 on v2

--- a/solution.py
+++ b/solution.py
@@ -66,13 +66,14 @@
         return (((y + step + NY) % NY) * NX + x, col)
 
     load_p = [
-        pltpu.make_async_copy(p_hbm.at[0, :, pl.ds(n * T, T)], pc.at[n, row], load_sem.at[n]) for n in range(2)
+        pltpu.make_async_copy(p_hbm.at[0, pl.ds((f * 2 + q) * QUART, QUART), pl.ds(n * T, T)], pc.at[n, y, x, f, q], load_sem.at[(n * 2 + f) * 2 + q])
+        for n in range(2) for f in range(2) for q in range(2)
     ]
     for c in load_p:
         c.start()
-    load_cols = pltpu.make_async_copy(cols_hbm, cols, load_sem.at[3])
+    load_cols = pltpu.make_async_copy(cols_hbm, cols, load_sem.at[9])
     load_cols.start()
-    load_a = pltpu.make_async_copy(a_hbm, a, load_sem.at[2])
+    load_a = pltpu.make_async_copy(a_hbm, a, load_sem.at[8])
     load_a.start()
 
     barrier = pltpu.get_barrier_semaphore()
@@ -81,8 +82,9 @@
         pl.semaphore_signal(barrier, inc=1, device_id=dev, device_id_type=MESH)
     for e in range(2):
         run[e, NSLOT] = jnp.zeros((T, T), F32)
-        load_p[e].wait()
-        pt[e, col] = pc[e, row].T
+        for c in load_p[4 * e:4 * e + 4]:
+            c.wait()
+        pt[e, col] = pc[e, y, x].reshape(T, T).T
     pl.semaphore_wait(barrier, len(partners))
 
     result = []
@@ -99,6 +101,10 @@
         c = copy(*args, **kw)
         c.start()
         into.append(c)
+
+    def drain(keep):
+        while len(late) > keep:
+            late.pop(0).wait_send()
 
     def zmsg(e, d, hop, q, recv):
         sign = 1 - 2 * d
@@ -128,22 +134,41 @@
         for shift in shifts:
             copy(*hmsg(e, shift, True)).wait_recv()
 
+    def wmsg(n, stage, axis, d, recv):
+        sign = 1 - 2 * d
+        back = (1 if stage % 2 == 0 else 2) if recv else stage % 2
+        along = ((x if axis == 0 else y) - sign * back + 2 * NX) % NX
+        across = slice(None) if stage >= 2 else (y if axis == 0 else x)
+        half = axis if stage < 2 else 1 - axis
+        ref = pc.at[n, across, along, half] if axis == 0 else pc.at[n, along, across, half]
+        if stage % 2 == 1:
+            ref = ref.at[d] if stage == 1 else ref.at[:, d]
+        i = (stage * 2 + axis) * 2 + d
+        return ref, ws.at[i], wr.at[i], xdev(sign) if axis == 0 else ydev(sign)
+
+    def wsend(n, stage):
+        for axis in range(2):
+            for d in range(2):
+                send(late, *wmsg(n, stage, axis, d, False))
+
+    def wwait(n, stage):
+        for axis in range(2):
+            for d in range(2):
+                copy(*wmsg(n, stage, axis, d, True)).wait_recv()
+
     names = {}
 
     def step_of(axis, amount):
         return (0, amount) if axis == 0 else (amount, 0)
 
-    def wgo(name, axis, d, offset, rows, recv):
+    def wgo(name, axis, d, offset, part, recv):
         sign = 1 - 2 * d
         dy, dx = offset
         if recv:
             sy, sx = step_of(axis, -sign)
             dy, dx = dy + sy, dx + sx
-        tile = ((y + dy + 2 * NY) % NY) * NX + (x + dx + 2 * NX) % NX
-        ref = pc.at[name[0], tile]
-        if rows is not None:
-            ref = ref.at[pl.ds(*rows)]
-        i = names.setdefault((axis, d) + name, len(names))
+        ref = pc.at[(0, (y + dy + 2 * NY) % NY, (x + dx + 2 * NX) % NX) + part]
+        i = 16 + names.setdefault((axis, d) + name, len(names))
         m = (ref, ws.at[i], wr.at[i], xdev(sign) if axis == 0 else ydev(sign))
         if recv:
             copy(*m).wait_recv()
@@ -152,24 +177,24 @@
 
     both = [(axis, d) for axis in range(2) for d in range(2)]
 
-    def w_own(n, recv):
+    def w_own(recv):
         for axis, d in both:
-            wgo((n, "own"), axis, d, (0, 0), None, recv)
-
-    def w_line2(n, recv):
+            wgo(("own",), axis, d, (0, 0), (), recv)
+
+    def w_line2(recv):
         for axis, d in both:
             for f in range(2):
-                wgo((n, "line2", f), axis, d, step_of(axis, 2 * d - 1), (f * HALF + d * QUART, QUART), recv)
-
-    def w_diag(n, o, recv):
+                wgo(("line2", f), axis, d, step_of(axis, 2 * d - 1), (f, d), recv)
+
+    def w_diag(o, recv):
         for axis, d in both:
-            wgo((n, "diag", o), axis, d, step_of(1 - axis, o), ((1 - axis) * HALF, HALF), recv)
-
-    def w_diag2(n, o, recv):
+            wgo(("diag", o), axis, d, step_of(1 - axis, o), (1 - axis,), recv)
+
+    def w_diag2(o, recv):
         for axis, d in both:
             ay, ax = step_of(axis, 2 * d - 1)
             by, bx = step_of(1 - axis, o)
-            wgo((n, "diag2", o), axis, d, (ay + by, ax + bx), ((1 - axis) * HALF + d * QUART, QUART), recv)
+            wgo(("diag2", o), axis, d, (ay + by, ax + bx), (1 - axis, d), recv)
 
     def left(e, dist, lo, hi):
         @pl.loop(lo, hi)
@@ -182,7 +207,7 @@
 
     def product(e, n, block):
         last = link_ref[block, SLOTS]
-        return jnp.dot(run[e, last].astype(BF16), pc[n, block], preferred_element_type=F32)
+        return jnp.dot(run[e, last].astype(BF16), pc[n, block // NX, block % NX].reshape(T, T), preferred_element_type=F32)
 
     def block_of(shift, k):
         return ((z + shift + NZ) % NZ) * 2 + k
@@ -252,32 +277,34 @@
     zsend(0, 0, 0)
     zsend(0, 0, 1)
     hsend(0, 0)
-    w_own(0, False)
+    w_own(False)
     zsend(1, 0, 0)
     zsend(1, 0, 1)
     hsend(1, 0)
     load_cols.wait()
     chain(cols, links, z, core)
-    to_scalars = pltpu.make_async_copy(links, link_ref, load_sem.at[4])
+    to_scalars = pltpu.make_async_copy(links, link_ref, load_sem.at[10])
     to_scalars.start()
     load_a.wait()
     to_scalars.wait()
+    hwait(0, 0)
+    left(0, 0, 0, 2)
     zwait(0, 0, 0)
     zsend(0, 1, 0)
     zwait(0, 0, 1)
     zsend(0, 1, 1)
     hsend(0, 1, -1)
-    w_own(0, True)
-    w_line2(0, False)
-    w_diag(0, -1, False)
-    w_diag(0, 1, False)
+    w_own(True)
+    w_line2(False)
+    w_diag(-1, False)
+    w_diag(1, False)
     zwait(1, 0, 0)
     zsend(1, 1, 0)
     zwait(1, 0, 1)
     zsend(1, 1, 1)
     hsend(1, 1, -1)
-    hwait(0, 0)
-    left(0, 0, 0, 2)
+    hwait(0, 1, -1)
+    left(0, 1, 0, 4)
     hwait(1, 0)
     left(1, 0, 0, 2)
     zwait(0, 1, 0)
@@ -285,89 +312,81 @@
     zwait(0, 1, 1)
     zsend(0, 2, 1)
     hsend(0, 2, -2)
-    w_line2(0, True)
-    w_diag(0, 2, False)
-    w_own(1, False)
-    hwait(0, 1, -1)
-    left(0, 1, 0, 4)
+    w_line2(True)
+    w_diag(2, False)
+    wsend(1, 0)
+    hwait(1, 1, -1)
+    left(1, 1, 0, 4)
     zwait(1, 1, 0)
     zsend(1, 2, 0)
     zwait(1, 1, 1)
     zsend(1, 2, 1)
     hsend(1, 2, -2)
-    w_diag(0, -1, True)
-    w_diag(0, 1, True)
-    w_diag2(0, -1, False)
-    w_diag2(0, 1, False)
-    hwait(1, 1, -1)
-    left(1, 1, 0, 4)
+    w_diag(-1, True)
+    w_diag(1, True)
+    w_diag2(-1, False)
+    w_diag2(1, False)
+    hwait(0, 2, -2)
+    left(0, 2, 0, 4)
     zwait(0, 2, 0)
     zsend(0, 3, 0)
-    w_diag(0, 2, True)
-    w_diag2(0, 2, False)
     zwait(0, 2, 1)
     hsend(0, 3, -3)
-    hwait(0, 2, -2)
-    left(0, 2, 0, 4)
+    w_diag(2, True)
+    w_diag2(2, False)
+    wwait(1, 0)
+    wsend(1, 1)
+    hwait(1, 2, -2)
+    left(1, 2, 0, 4)
+    hwait(0, 3, -3)
+    left(0, 3, 0, 4)
     zwait(1, 2, 0)
     zsend(1, 3, 0)
     zwait(1, 2, 1)
     hsend(1, 3, -3)
-    hwait(0, 3, -3)
-    left(0, 3, 0, 4)
     zwait(0, 3, 0)
     hsend(0, 4)
     left(0, 4, 0, 1)
-    w_diag2(0, -1, True)
-    w_diag2(0, 1, True)
-    w_diag2(0, 2, True)
     hwait(0, 4)
     left(0, 4, 1, 2)
     for c in held[0]:
         c.wait_send()
+    w_diag2(-1, True)
+    w_diag2(1, True)
+    w_diag2(2, True)
     exchange(0, 4, 3, -3)
-    hwait(1, 2, -2)
-    left(1, 2, 0, 4)
+    hwait(1, 3, -3)
+    left(1, 3, 0, 2)
     ring(0, 0)
     ring(0, 1)
+    wwait(1, 1)
+    wsend(1, 2)
     zwait(1, 3, 0)
     hsend(1, 4)
-    hwait(1, 3, -3)
-    left(1, 3, 0, 4)
+    left(1, 3, 2, 4)
     left(1, 4, 0, 1)
     hwait(1, 4)
     left(1, 4, 1, 2)
     for c in held[1]:
         c.wait_send()
     exchange(1, 4, 3, -3)
-    w_own(1, True)
-    w_line2(1, False)
-    w_diag(1, -1, False)
-    w_diag(1, 1, False)
+
     exchange(0, 2, -2)
     ring(1, 0)
     ring(1, 1)
     ring(0, 2)
     ring(0, 3)
     exchange(1, 2, -2)
-    w_line2(1, True)
-    w_diag(1, 2, False)
     exchange(0, 1, -1)
     ring(1, 2)
     ring(1, 3)
-    w_diag(1, -1, True)
-    w_diag(1, 1, True)
-    w_diag2(1, -1, False)
-    w_diag2(1, 1, False)
+    wwait(1, 2)
+    wsend(1, 3)
     ring(0, 4)
-    w_diag(1, 2, True)
-    w_diag2(1, 2, False)
     exchange(1, 1, -1)
     ring(0, 5)
     ring(0, 6)
-    w_diag2(1, -1, True)
-    w_diag2(1, 1, True)
-    w_diag2(1, 2, True)
+    wwait(1, 3)
 
     exchange(2, 4, 3, -3)
     ring(1, 4)
@@ -404,8 +423,7 @@
     ring(3, 7)
     ring(2, 8)
     ring(3, 8)
-    for c in late:
-        c.wait_send()
+    drain(0)
     for c in result:
         c.wait()
 
@@ -426,7 +444,7 @@
             pltpu.VMEM((2, NSLOT + 1, T, T), F32),
             pltpu.VMEM((NSLOT, T, T), BF16),
             pltpu.VMEM((2, ROWS, T, T), BF16),
-            pltpu.VMEM((2, ROWS, T, T), BF16),
+            pltpu.VMEM((2, NY, NX, 2, 2, QUART, T), BF16),
             pltpu.VMEM((32, T, T), BF16),
             pltpu.VMEM((32, T, T), BF16),
             pltpu.VMEM((8, T, T), BF16),
@@ -434,10 +452,10 @@
             pltpu.VMEM((SLOTS, ROWS), jnp.int32),
             pltpu.VMEM((ROWS, 128), jnp.int32),
             pltpu.SMEM((ROWS, 128), jnp.int32),
-            dma((5,)), dma((4,)),
+            dma((11,)), dma((4,)),
             dma((32,)), dma((32,)),
             dma((16,)), dma((16,)),
-            dma((72,)), dma((72,)),
+            dma((52,)), dma((52,)),
             dma((32,)), dma((32,)),
             dma((64,)), dma((64,)),
         ],

time: 84.5 us -> 82.7 us (0.979)
  Pallas kernels: 82.1 us -> 80.3 us
    pallas_call x1, Pallas kernels: 82.1 us -> 80.3 us  [per_device(): pl.pallas_call(kernel, out_shape=jax.ShapeDtypeStruct((2 * T, 2 * T), F32...]
where the time goes in v3:
time: 82.7 us; the launch traced here: 82.6 us
  Pallas kernels  80.3 us (97%)
  local copies, waits for them, and re-layouts  2.26 us (3%)
    pallas_call x1, Pallas kernels, per_device(): pl.pallas_call(kernel, out_shape=jax.ShapeDtypeStruct((2 * T, 2 * T), F32...  80.3 us
    unnamed x1, local copies, waits for them, and re-layouts  2.26 us

profile of v3, /device:TPU:1, one launch (start us, length us, event | category | flops | bytes accessed | tf_op | source)
XLA Modules:
  0.0 82.6 jit_solution(13562802743357861983)
XLA Ops:
  0.0 80.3 %shard_map.37 = f32[512,512]{1,0:T(8,128)} custom-call(s32[4,16]{1,0:T(4,128)} %bitcast.3, bf16[64,256,256]{2,1,0:T(8,128)(2,1)} %bitcast.2, bf16[1,256,512]{2,1,0:T(8,128)(2,1)} %p_hbm.1), custom_call_target="tpu_custom_call" | custom-call | flops 6442450944 | bytes 10000000 | tf_op jit(solution)/shard_map/pallas_call | solution.py:433
  80.3 2.3 %copy.5 = f32[512,512]{1,0:T(8,128)} copy(f32[512,512]{1,0:T(8,128)} %shard_map.37) | data formatting | bytes 2097152

commit v4 on v3

--- a/solution.py
+++ b/solution.py
@@ -370,10 +370,9 @@
     for c in held[1]:
         c.wait_send()
     exchange(1, 4, 3, -3)
-
-    exchange(0, 2, -2)
     ring(1, 0)
     ring(1, 1)
+    exchange(0, 2, -2)
     ring(0, 2)
     ring(0, 3)
     exchange(1, 2, -2)
@@ -387,7 +386,6 @@
     ring(0, 5)
     ring(0, 6)
     wwait(1, 3)
-
     exchange(2, 4, 3, -3)
     ring(1, 4)
     ring(2, 0)
@@ -428,9 +426,22 @@
         c.wait()
 
 
+def hand_over(src, dst, via, into, out):
+    parts = [pl.ds(i * QUART, QUART) for i in range(8)]
+    come = [pltpu.make_async_copy(src.at[r], via.at[r], into.at[i]) for i, r in enumerate(parts)]
+    go = [pltpu.make_async_copy(via.at[r], dst.at[r], out.at[i]) for i, r in enumerate(parts)]
+    for c in come:
+        c.start()
+    for c, g in zip(come, go):
+        c.wait()
+        g.start()
+    for g in go:
+        g.wait()
+
+
 def per_device(a_vals, a_cols, p_vals):
     dma = pltpu.SemaphoreType.DMA
-    return pl.pallas_call(
+    coarse = pl.pallas_call(
         kernel,
         out_shape=jax.ShapeDtypeStruct((2 * T, 2 * T), F32),
         in_specs=[
@@ -464,6 +475,13 @@
         ),
         cost_estimate=pl.CostEstimate(flops=6_442_450_944, bytes_accessed=10_000_000, transcendentals=0),
     )(a_cols.T, a_vals.reshape(NSLOT, T, T), p_vals)
+    return pl.pallas_call(
+        hand_over,
+        out_shape=jax.ShapeDtypeStruct((2 * T, 2 * T), F32),
+        in_specs=[pl.BlockSpec(memory_space=pl.ANY)],
+        out_specs=pl.BlockSpec(memory_space=pl.ANY),
+        scratch_shapes=[pltpu.VMEM((2 * T, 2 * T), F32), dma((8,)), dma((8,))],
+    )(coarse)
 
 
 def solution(mesh):

time: 82.7 us -> 82.7 us (level)
  local copies, waits for them, and re-layouts: 2.26 us -> 0 us
  Pallas kernels: 80.3 us -> 82.4 us
    unnamed x1 -> x0, local copies, waits for them, and re-layouts: 2.26 us -> none
    pallas_call x0 -> x1, Pallas kernels: none -> 2.09 us  [per_device(): pl.pallas_call(hand_over, out_shape=jax.ShapeDtypeStruct((2 * T, 2 * T),...]
where the time goes in v4:
time: 82.7 us; the launch traced here: 82.6 us
  Pallas kernels  82.4 us (100%)
    pallas_call x1, Pallas kernels, per_device(): pl.pallas_call(kernel, out_shape=jax.ShapeDtypeStruct((2 * T, 2 * T), F32...  80.3 us
    pallas_call x1, Pallas kernels, per_device(): pl.pallas_call(hand_over, out_shape=jax.ShapeDtypeStruct((2 * T, 2 * T),...  2.09 us

profile of v4, /device:TPU:1, one launch (start us, length us, event | category | flops | bytes accessed | tf_op | source)
XLA Modules:
  0.0 82.6 jit_solution(930440424421451956)
XLA Ops:
  0.0 80.3 %shard_map.37.src = f32[512,512]{1,0:T(8,128)} custom-call(s32[4,16]{1,0:T(4,128)} %bitcast.3, bf16[64,256,256]{2,1,0:T(8,128)(2,1)} %bitcast.2, bf16[1,256,512]{2,1,0:T(8,128)(2,1)} %p_hbm.1), custom_call_target="tpu_custom_call" | custom-call | flops 6442450944 | bytes 10000000 | tf_op jit(solution)/shard_map/pallas_call | solution.py:444
  80.3 2.1 %shard_map.38 = f32[512,512]{1,0:T(8,128)} custom-call(f32[512,512]{1,0:T(8,128)} %shard_map.37.src), custom_call_target="tpu_custom_call" | custom-call | tf_op jit(solution)/shard_map/pallas_call | solution.py:478
